TPU v7x, 32 devices: a whole 2x2x4 slice. The times are simulated.
32 devices in a mesh: gx: 8 (over z, y), gy: 4 (over x, core).
Axes of the slice: x: 2, y: 2, z: 4, core: 2. Of those that a mesh axis runs over, the one named last changes fastest.
Arguments:
- cell_means: float32 [30, 32, 16, 128], P(None, 'gx', 'gy'), may hold values from 0 to 1
- diffusion: float32 [32, 16, 128], P('gx', 'gy'), may hold values from 0.02 to 0.15
- mix_rate: float32 [32, 16, 128], P('gx', 'gy'), may hold values from 0.05 to 3
- send_lists: int32 [32, 32, 128], P(('gx', 'gy')), may hold values from 0 to 2047
- compositions: float32 [30, 131072], P(None, ('gx', 'gy')), may hold values from 0 to 1
- weights: float32 [131072], P(('gx', 'gy')), may hold values from 0.5 to 2
- particle_slots: int32 [131072], P(('gx', 'gy')), may hold values from 0 to 4095
- partners: int32 [131072], P(('gx', 'gy')), may hold values from 0 to 4095
Outputs:
- new_means: float32 [30, 32, 16, 128], P(None, 'gx', 'gy')
- new_compositions: float32 [30, 131072], P(None, ('gx', 'gy'))
Inputs may be any that keep to these rules, and one draw needn't show every extreme that they name: particle_slots = s * 128 + r names slot r of the list that tile s sends to the particle's device.
All inputs are finite; a program needn't handle non-finite values.
Results may differ from a plain program's by a relative error of at most 0.00002.
Values sent between devices are 32-bit elements; how exact they have to be, the bound alone decides.
A program may use at most 64 MiB of HBM per device.

v0:
```python
import jax
import jax.numpy as jnp
from jax import lax
from jax.sharding import PartitionSpec as P

PAIR_RATE = 0.3


def with_halo(shard, sides, width):
    for axis, dim in sides:
        devices, length = (lax.axis_size(axis), shard.shape[dim])
        up = [(i, (i + 1) % devices) for i in range(devices - 1)]
        down = [(j, i) for i, j in up]
        last = lax.slice_in_dim(shard, length - width, length, axis=dim)
        initial = lax.slice_in_dim(shard, 0, width, axis=dim)
        before = lax.ppermute(last, axis, up)
        after = lax.ppermute(initial, axis, down)
        shard = jnp.concatenate([before, shard, after], axis=dim)
    return shard


def on_device(
    cell_means, diffusion, mix_rate, send_lists, compositions, weights, particle_slots, partners
):
    species, rows_x, rows_y, depth = cell_means.shape
    cell_count = rows_x * rows_y * depth
    groups_x = lax.axis_size("gx")
    groups_y = lax.axis_size("gy")
    padded = with_halo(cell_means, (("gx", 1), ("gy", 2)), 1)
    deepened = jnp.pad(cell_means, ((0, 0), (0, 0), (0, 0), (1, 1)))
    neighbours = (
        padded[:, 2:, 1:-1] + padded[:, :-2, 1:-1] + padded[:, 1:-1, 2:] + padded[:, 1:-1, :-2]
    )
    neighbours = neighbours + deepened[:, :, :, 2:] + deepened[:, :, :, :-2]
    filtered = cell_means + diffusion[None] * (neighbours - 6.0 * cell_means)
    fields = jnp.concatenate(
        [filtered.reshape(species, cell_count), mix_rate.reshape(1, cell_count)], 0
    )
    slots_peer = send_lists.shape[2]
    slot_count = groups_x * groups_y * slots_peer
    flat_list = send_lists[0].reshape(-1)
    outgoing = jnp.take(fields, flat_list, axis=1)
    received = lax.all_to_all(outgoing, ("gx", "gy"), split_axis=1, concat_axis=1, tiled=True)
    local_means = jnp.take(received, particle_slots, axis=1)
    mates = jnp.take(compositions, partners, axis=1)
    blend_rate = 1.0 - jnp.exp(-local_means[species])
    new_compositions = (
        compositions
        - blend_rate[None] * (compositions - local_means[:species])
        - PAIR_RATE * (compositions - mates)
    )
    weighted = jnp.concatenate([weights[None] * new_compositions, weights[None]], 0)
    moments = jnp.zeros((species + 1, slot_count), jnp.float32).at[:, particle_slots].add(weighted)
    returned = lax.all_to_all(moments, ("gx", "gy"), split_axis=1, concat_axis=1, tiled=True)
    totals = jnp.zeros((species + 1, cell_count), jnp.float32).at[:, flat_list].add(returned)
    updated = (totals[:species] + fields[:species]) / (totals[species][None] + 1.0)
    return (updated.reshape(species, rows_x, rows_y, depth), new_compositions)


def solution(mesh):
    in_specs = (
        P(None, "gx", "gy", None),
        P("gx", "gy", None),
        P("gx", "gy", None),
        P(("gx", "gy"), None, None),
        P(None, ("gx", "gy")),
        P(("gx", "gy")),
        P(("gx", "gy")),
        P(("gx", "gy")),
    )
    out_specs = (P(None, "gx", "gy", None), P(None, ("gx", "gy")))
    return jax.shard_map(
        on_device, mesh=mesh, in_specs=in_specs, out_specs=out_specs, check_vma=False
    )
```

profile of v0, /device:TPU:0, one launch (start us, length us, event | category | flops | bytes accessed | tf_op | source)
XLA Modules:
  0.0 158.9 jit_solution(12772471050581777557)
XLA Ops:
  0.7 0.9 fusion.23
  1.6 4.9 %collective-permute-start.1 = (f32[30,1,4,128]{3,2,1,0:T(4,128)S(1)}, f32[30,1,4,128]{3,2,1,0:T(4,128)S(1)}, u32[]{:S(2)}, u32[]{:S(2)}) collective-permute-start(f32[30,1,4,128]{3,2,1,0:T(4,128)S(1)} %get-tuple-element.19), channel_id=1, source_target_pairs={{0,4},{4,8},{8,12},{12,16},{16,20},{20,24},{24,28},{1,5},{5,9},{9,... | collective-permute-start | bytes 184328 | tf_op jit(solution)/shard_map/ppermute | solution.py:16
  6.4 1.3 collective-permute-start
  7.7 0.7 compare_select_fusion
  8.5 1.0 constant_dynamic-update-slice_fusion.1
  9.5 3.0 %collective-permute-done = f32[30,1,4,128]{3,2,1,0:T(4,128)S(1)} collective-permute-done((f32[30,1,4,128]{3,2,1,0:T(4,128)S(1)}, f32[30,1,4,128]{3,2,1,0:T(4,128)S(1)}, u32[]{:S(2)}, u32[]{:S(2)}) %collective-permute-start) | collective-permute-done | bytes 61472 | tf_op jit(solution)/shard_map/ppermute | solution.py:17
  12.7 1.3 collective-permute-start.3
  14.0 1.3 collective-permute-start.2
  15.3 0.7 compare_and_fusion.1
  16.1 1.1 copy.72
  17.1 1.8 %collective-permute-done.2 = f32[30,6,1,128]{3,2,1,0:T(1,128)S(1)} collective-permute-done((f32[30,6,1,128]{3,2,1,0:T(1,128)S(1)}, f32[30,6,1,128]{3,2,1,0:T(1,128)S(1)}, u32[]{:S(2)}, u32[]{:S(2)}) %collective-permute-start.2) | collective-permute-done | bytes 92192 | tf_op jit(solution)/shard_map/ppermute | solution.py:17
  19.0 0.4 fusion.14
  19.4 0.4 copy.71
  20.1 14.2 %gather_fusion = f32[4096,31]{1,0:T(8,128)} fusion(f32[31,2048]{0,1:T(8,128)S(1)} %pad_maximum_fusion, s32[4096]{0:T(1024)S(1)} %broadcast_clamp_fusion.1), kind=kCustom, calls=%fused_computation | custom fusion | bytes 1032192 | tf_op jit(solution)/shard_map/jit(_take)/gather | solution.py:42
  34.3 2.2 %copy.73 = f32[31,32,128]{2,0,1:T(8,128)S(1)} copy(f32[31,32,128]{0,2,1:T(8,128)} %bitcast.37) | data formatting | bytes 1015808 | tf_op jit(solution)/shard_map/jit(_take)/gather | solution.py:42
  36.5 0.9 broadcast_select_fusion
  37.4 7.7 %all-to-all-start = ((f32[31,32,128]{2,0,1:T(8,128)}), f32[31,32,128]{2,0,1:T(8,128)}, u32[]{:S(2)}, u32[]{:S(2)}) async-start(f32[31,32,128]{2,0,1:T(8,128)} %broadcast_select_fusion), calls=%async_computation | async-start | bytes 1048576 | tf_op jit(solution)/shard_map/all_to_all | solution.py:43
  45.1 1.7 %copy.76 = f32[30,4096]{0,1:T(8,128)S(1)} copy(f32[30,4096]{1,0:T(8,128)} %param.12) | data formatting | bytes 983040 | tf_op args[4]
  46.8 14.2 %gather_fusion.2 = f32[4096,30]{1,0:T(8,128)} fusion(f32[30,4096]{0,1:T(8,128)S(1)} %copy.76, s32[4096]{0:T(1024)S(1)} %fusion.20), kind=kCustom, calls=%fused_computation.2 | custom fusion | bytes 999424 | tf_op jit(solution)/shard_map/jit(_take)/gather | solution.py:45
  61.0 3.0 %copy.77 = f32[4096,30]{0,1:T(8,128)} copy(f32[4096,30]{1,0:T(8,128)} %gather_fusion.2) | data formatting | bytes 983040 | tf_op jit(solution)/shard_map/jit(_take)/gather | solution.py:45
  64.1 1.7 %copy.74 = f32[31,32,128]{0,2,1:T(8,128)S(1)} copy(f32[31,32,128]{2,0,1:T(8,128)} %all-to-all-done) | data formatting | bytes 1015808 | tf_op jit(solution)/shard_map/all_to_all | solution.py:43
  65.7 14.2 %gather_fusion.1 = f32[4096,31]{1,0:T(8,128)} fusion(f32[31,4096]{0,1:T(8,128)S(1)} %bitcast.33, s32[4096]{0:T(1024)S(1)} %get-tuple-element.20), kind=kCustom, calls=%fused_computation.1 | custom fusion | bytes 1032192 | tf_op jit(solution)/shard_map/jit(_take)/gather | solution.py:44
  79.9 2.3 %copy.75 = f32[4096,31]{0,1:T(8,128)S(1)} copy(f32[4096,31]{1,0:T(8,128)} %gather_fusion.1) | data formatting | bytes 1015808 | tf_op jit(solution)/shard_map/jit(_take)/gather | solution.py:44
  82.4 0.9 broadcast_multiply_fusion
  83.3 2.0 %copy.78 = f32[4096,31]{1,0:T(8,128)} copy(f32[4096,31]{0,1:T(8,128)S(1)} %maximum_bitcast_fusion) | data formatting | bytes 1015808 | tf_op jit(solution)/shard_map/concatenate | solution.py:52
  85.4 23.2 %scatter_custom_fusion = f32[31,4096]{0,1:T(8,128)S(1)} fusion(s32[4096]{0:T(1024)S(1)} %get-tuple-element.21, f32[4096,31]{1,0:T(8,128)} %copy.78, f32[]{:T(128)} %constant.25.clone.1), kind=kCustom, calls=%fused_computation.10 | custom fusion | flops 126976 | bytes 508416 | tf_op jit(solution)/shard_map/scatter-add | solution.py:53
  108.5 1.4 copy.79
  110.0 21.3 %all_to_all.21 = f32[31,32,128]{2,0,1:T(8,128)S(1)} all-to-all(f32[31,32,128]{2,0,1:T(8,128)} %copy.79), channel_id=1, replica_groups=mesh['gx'=8,'gy'=4] {'gx','gy'}, dimensions={1} | all-to-all | bytes 1015808 | tf_op jit(solution)/shard_map/all_to_all | solution.py:54
  131.9 2.0 %copy.81 = f32[4096,31]{1,0:T(8,128)} copy(f32[4096,31]{0,1:T(8,128)S(1)} %bitcast.38) | data formatting | bytes 1015808 | tf_op jit(solution)/shard_map/all_to_all | solution.py:54
  133.9 22.9 %scatter_custom_fusion.1 = f32[31,2048]{0,1:T(8,128)S(1)} fusion(s32[4096]{0:T(1024)S(1)} %bitcast.42, f32[4096,31]{1,0:T(8,128)} %copy.81, f32[]{:T(128)} %constant.25.clone.1), kind=kCustom, calls=%fused_computation.22 | custom fusion | flops 126976 | bytes 254464 | tf_op jit(solution)/shard_map/scatter-add | solution.py:55
  156.8 0.6 fusion
  157.8 1.0 copy.82
  (33 shorter events, 1.7 us)
Async XLA Ops:
  0.6 18.3 %copy-start.2 = (f32[30,4,4,128]{3,2,1,0:T(4,128)S(1)}, f32[30,4,4,128]{3,2,1,0:T(4,128)}, u32[]{:S(2)}) copy-start(f32[30,4,4,128]{3,2,1,0:T(4,128)} %param.8) | copy-start | bytes 737284
  0.6 18.3 %copy-start.6 = (f32[4,4,128]{2,1,0:T(4,128)S(1)}, f32[4,4,128]{2,1,0:T(4,128)}, u32[]{:S(2)}) copy-start(f32[4,4,128]{2,1,0:T(4,128)} %param.9) | copy-start | bytes 24580
  1.6 6.9 %collective-permute-start.1 = (f32[30,1,4,128]{3,2,1,0:T(4,128)S(1)}, f32[30,1,4,128]{3,2,1,0:T(4,128)S(1)}, u32[]{:S(2)}, u32[]{:S(2)}) collective-permute-start(f32[30,1,4,128]{3,2,1,0:T(4,128)S(1)} %get-tuple-element.19), channel_id=1, source_target_pairs={{0,4},{4,8},{8,12},{12,16},{16,20},{20,24},{24,28},{1,5},{5,9},{9,... | collective-permute-start | bytes 184328 | tf_op jit(solution)/shard_map/ppermute | solution.py:16
  6.4 6.1 %collective-permute-start = (f32[30,1,4,128]{3,2,1,0:T(4,128)S(1)}, f32[30,1,4,128]{3,2,1,0:T(4,128)S(1)}, u32[]{:S(2)}, u32[]{:S(2)}) collective-permute-start(f32[30,1,4,128]{3,2,1,0:T(4,128)S(1)} %get-tuple-element.18), channel_id=1, source_target_pairs={{4,0},{8,4},{12,8},{16,12},{20,16},{24,20},{28,24},{5,1},{9,5},{13... | collective-permute-start | bytes 184328 | tf_op jit(solution)/shard_map/ppermute | solution.py:17
  12.7 4.4 %collective-permute-start.3 = (f32[30,6,1,128]{3,2,1,0:T(1,128)S(1)}, f32[30,6,1,128]{3,2,1,0:T(1,128)S(1)}, u32[]{:S(2)}, u32[]{:S(2)}) collective-permute-start(f32[30,6,1,128]{3,2,1,0:T(1,128)S(1)} %get-tuple-element.17), channel_id=1, source_target_pairs={{0,1},{1,2},{2,3},{4,5},{5,6},{6,7},{8,9},{9,10},{10,11},{12,13},{... | collective-permute-start | bytes 276488 | tf_op jit(solution)/shard_map/ppermute | solution.py:16
  14.0 4.9 %collective-permute-start.2 = (f32[30,6,1,128]{3,2,1,0:T(1,128)S(1)}, f32[30,6,1,128]{3,2,1,0:T(1,128)S(1)}, u32[]{:S(2)}, u32[]{:S(2)}) collective-permute-start(f32[30,6,1,128]{3,2,1,0:T(1,128)S(1)} %get-tuple-element.16), channel_id=1, source_target_pairs={{1,0},{2,1},{3,2},{5,4},{6,5},{7,6},{9,8},{10,9},{11,10},{13,12},{... | collective-permute-start | bytes 276488 | tf_op jit(solution)/shard_map/ppermute | solution.py:17
  37.4 9.4 %copy-start.4 = (s32[4096]{0:T(1024)S(1)}, s32[4096]{0:T(1024)}, u32[]{:S(2)}) copy-start(s32[4096]{0:T(1024)} %param.15) | copy-start | bytes 49156
  37.4 26.7 %all-to-all-start = ((f32[31,32,128]{2,0,1:T(8,128)}), f32[31,32,128]{2,0,1:T(8,128)}, u32[]{:S(2)}, u32[]{:S(2)}) async-start(f32[31,32,128]{2,0,1:T(8,128)} %broadcast_select_fusion), calls=%async_computation | async-start | bytes 1048576 | tf_op jit(solution)/shard_map/all_to_all | solution.py:43
  61.0 3.0 %copy-start.3 = (s32[4096]{0:T(1024)S(1)}, s32[4096]{0:T(1024)}, u32[]{:S(2)}) copy-start(s32[4096]{0:T(1024)} %param.14) | copy-start | bytes 49156
  79.9 2.4 %copy-start = (f32[30,4096]{1,0:T(8,128)S(1)}, f32[30,4096]{1,0:T(8,128)}, u32[]{:S(2)}) copy-start(f32[30,4096]{1,0:T(8,128)} %param.12) | copy-start | bytes 1474564
  79.9 2.4 %copy-start.1 = (f32[4096,30]{0,1:T(8,128)S(1)}, f32[4096,30]{0,1:T(8,128)}, u32[]{:S(2)}) copy-start(f32[4096,30]{0,1:T(8,128)} %copy.77) | copy-start | bytes 1474564
  79.9 2.4 %copy-start.5 = (f32[4096]{0:T(1024)S(1)}, f32[4096]{0:T(1024)}, u32[]{:S(2)}) copy-start(f32[4096]{0:T(1024)} %param.13) | copy-start | bytes 49156
where the time goes:
time: 160 us; the launch traced here: 159 us
  local copies, waits for them, and re-layouts  64 us (40%)
  other arithmetic  51.3 us (32%)
  blocking collectives  21.3 us (13%)
  starting transfers between devices  16.5 us (10%)
  waiting for transfers between devices  4.86 us (3%)
    scatter-add x1, other arithmetic, on_device(): jnp.zeros((species + 1, slot_count), jnp.float32).at[:, particle_slots]  23.2 us
    scatter-add x1, other arithmetic, on_device(): jnp.zeros((species + 1, cell_count), jnp.float32).at[:, flat_list]  22.9 us
    all_to_all x1, blocking collectives, on_device(): lax.all_to_all(moments, ('gx', 'gy'), split_axis=1, concat_axis=1, tiled=...  21.3 us
    gather x2, local copies, waits for them, and re-layouts, on_device(): mates = jnp.take(compositions, partners, axis=1)  17.2 us
    gather x2, local copies, waits for them, and re-layouts, on_device(): local_means = jnp.take(received, particle_slots, axis=1)  16.5 us
    gather x2, local copies, waits for them, and re-layouts, on_device(): outgoing = jnp.take(fields, flat_list, axis=1)  16.4 us
    all_to_all x1, starting transfers between devices, on_device(): lax.all_to_all(outgoing, ('gx', 'gy'), split_axis=1, concat_axis=1, tiled...  7.72 us
    ppermute x2, starting transfers between devices, with_halo(): before = lax.ppermute(last, axis, up)  6.17 us
  transfers between devices with their start and end apart: 5, of which 2 were waited for; matrix products, arithmetic and copies ran while one was open for 14% of the time, Pallas kernels for 0%

commit v1 on v0

--- a/solution.py
+++ b/solution.py
@@ -40,7 +40,9 @@
     slot_count = groups_x * groups_y * slots_peer
     flat_list = send_lists[0].reshape(-1)
     outgoing = jnp.take(fields, flat_list, axis=1)
-    received = lax.all_to_all(outgoing, ("gx", "gy"), split_axis=1, concat_axis=1, tiled=True)
+    shards = jnp.split(outgoing, lax.axis_size(("gx", "gy")), axis=1)
+    got = lax.all_to_all(jnp.stack(shards), ("gx", "gy"), 0, 0)
+    received = jnp.concatenate(got, axis=1)
     local_means = jnp.take(received, particle_slots, axis=1)
     mates = jnp.take(compositions, partners, axis=1)
     blend_rate = 1.0 - jnp.exp(-local_means[species])

time: 160 us -> 178 us (1.11)
  local copies, waits for them, and re-layouts: 64 us -> 83.1 us
    unnamed x20 -> x51, local copies, waits for them, and re-layouts: 4.07 us -> 22.7 us
  transfers between devices with their start and end apart: 5 -> 5, of which waited for: 2 -> 2; matrix products, arithmetic and copies ran while one was open for 14% -> 13% of each run, Pallas kernels for 0% -> 0%
where the time goes in v1:
time: 178 us; the launch traced here: 177 us
  local copies, waits for them, and re-layouts  83.1 us (47%)
  other arithmetic  51.2 us (29%)
  blocking collectives  21.3 us (12%)
  starting transfers between devices  16.5 us (9%)
  waiting for transfers between devices  4.14 us (2%)
    scatter-add x1, other arithmetic, on_device(): jnp.zeros((species + 1, slot_count), jnp.float32).at[:, particle_slots]  23.2 us
    scatter-add x1, other arithmetic, on_device(): jnp.zeros((species + 1, cell_count), jnp.float32).at[:, flat_list]  22.9 us
    unnamed x51, local copies, waits for them, and re-layouts  22.7 us
    all_to_all x1, blocking collectives, on_device(): lax.all_to_all(moments, ('gx', 'gy'), split_axis=1, concat_axis=1, tiled=...  21.3 us
    gather x2, local copies, waits for them, and re-layouts, on_device(): mates = jnp.take(compositions, partners, axis=1)  17.1 us
    gather x2, local copies, waits for them, and re-layouts, on_device(): local_means = jnp.take(received, particle_slots, axis=1)  16.4 us
    gather x2, local copies, waits for them, and re-layouts, on_device(): outgoing = jnp.take(fields, flat_list, axis=1)  16.3 us
    all_to_all x1, starting transfers between devices, on_device(): got = lax.all_to_all(jnp.stack(shards), ('gx', 'gy'), 0, 0)  7.72 us
  transfers between devices with their start and end apart: 5, of which 2 were waited for; matrix products, arithmetic and copies ran while one was open for 13% of the time, Pallas kernels for 0%

profile of v1, /device:TPU:0, one launch (start us, length us, event | category | flops | bytes accessed | tf_op | source)
XLA Modules:
  0.0 177.1 jit_solution(9691389291501184115)
XLA Ops:
  0.7 0.9 fusion.23
  1.6 4.9 %collective-permute-start.1 = (f32[30,1,4,128]{3,2,1,0:T(4,128)S(1)}, f32[30,1,4,128]{3,2,1,0:T(4,128)S(1)}, u32[]{:S(2)}, u32[]{:S(2)}) collective-permute-start(f32[30,1,4,128]{3,2,1,0:T(4,128)S(1)} %get-tuple-element.19), channel_id=1, source_target_pairs={{0,4},{4,8},{8,12},{12,16},{16,20},{20,24},{24,28},{1,5},{5,9},{9,... | collective-permute-start | bytes 184328 | tf_op jit(solution)/shard_map/ppermute | solution.py:16
  6.4 1.3 collective-permute-start
  7.7 0.7 compare_select_fusion
  8.5 0.7 fusion.20
  9.3 1.0 constant_dynamic-update-slice_fusion.1
  10.2 2.3 %collective-permute-done = f32[30,1,4,128]{3,2,1,0:T(4,128)S(1)} collective-permute-done((f32[30,1,4,128]{3,2,1,0:T(4,128)S(1)}, f32[30,1,4,128]{3,2,1,0:T(4,128)S(1)}, u32[]{:S(2)}, u32[]{:S(2)}) %collective-permute-start) | collective-permute-done | bytes 61472 | tf_op jit(solution)/shard_map/ppermute | solution.py:17
  12.7 1.3 collective-permute-start.3
  14.0 1.3 collective-permute-start.2
  15.3 0.7 compare_and_fusion.1
  16.1 1.1 copy.136
  17.1 1.8 %collective-permute-done.2 = f32[30,6,1,128]{3,2,1,0:T(1,128)S(1)} collective-permute-done((f32[30,6,1,128]{3,2,1,0:T(1,128)S(1)}, f32[30,6,1,128]{3,2,1,0:T(1,128)S(1)}, u32[]{:S(2)}, u32[]{:S(2)}) %collective-permute-start.2) | collective-permute-done | bytes 92192 | tf_op jit(solution)/shard_map/ppermute | solution.py:17
  20.1 14.1 %gather_fusion = f32[4096,31]{1,0:T(8,128)} fusion(f32[31,2048]{0,1:T(8,128)S(1)} %pad_maximum_fusion, s32[4096]{0:T(1024)S(1)} %get-tuple-element.23), kind=kCustom, calls=%fused_computation | custom fusion | bytes 1032192 | tf_op jit(solution)/shard_map/jit(_take)/gather | solution.py:42
  34.2 2.2 %copy.137 = f32[4096,31]{0,1:T(8,128)S(1)} copy(f32[4096,31]{1,0:T(8,128)} %gather_fusion) | data formatting | bytes 1015808 | tf_op jit(solution)/shard_map/jit(_take)/gather | solution.py:42
  36.5 0.6 constant_dynamic-update-slice_fusion.34
  46.7 0.6 constant_dynamic-update-slice_fusion.17
  55.8 7.7 %all-to-all-start = ((f32[32,31,128]{2,1,0:T(8,128)}), f32[32,31,128]{2,1,0:T(8,128)}, u32[]{:S(2)}, u32[]{:S(2)}) async-start(f32[32,31,128]{2,1,0:T(8,128)} %constant_dynamic-update-slice_fusion.3), calls=%async_computation | async-start | bytes 1048576 | tf_op jit(solution)/shard_map/all_to_all | solution.py:44
  63.5 1.7 copy.140
  65.2 14.1 %gather_fusion.2 = f32[4096,30]{1,0:T(8,128)} fusion(f32[30,4096]{0,1:T(8,128)S(1)} %copy.140, s32[4096]{0:T(1024)S(1)} %get-tuple-element.22), kind=kCustom, calls=%fused_computation.2 | custom fusion | bytes 999424 | tf_op jit(solution)/shard_map/jit(_take)/gather | solution.py:47
  79.3 3.0 %copy.141 = f32[4096,30]{0,1:T(8,128)} copy(f32[4096,30]{1,0:T(8,128)} %gather_fusion.2) | data formatting | bytes 983040 | tf_op jit(solution)/shard_map/jit(_take)/gather | solution.py:47
  82.4 1.7 copy.138
  84.0 14.1 %gather_fusion.1 = f32[4096,31]{1,0:T(8,128)} fusion(f32[31,4096]{0,1:T(8,128)S(1)} %bitcast.161, s32[4096]{0:T(1024)S(1)} %get-tuple-element.20), kind=kCustom, calls=%fused_computation.1 | custom fusion | bytes 1032192 | tf_op jit(solution)/shard_map/jit(_take)/gather | solution.py:46
  98.2 2.3 %copy.139 = f32[4096,31]{0,1:T(8,128)S(1)} copy(f32[4096,31]{1,0:T(8,128)} %gather_fusion.1) | data formatting | bytes 1015808 | tf_op jit(solution)/shard_map/jit(_take)/gather | solution.py:46
  100.6 0.9 broadcast_multiply_fusion
  101.6 2.0 %copy.142 = f32[4096,31]{1,0:T(8,128)} copy(f32[4096,31]{0,1:T(8,128)S(1)} %maximum_bitcast_fusion) | data formatting | bytes 1015808 | tf_op jit(solution)/shard_map/concatenate | solution.py:54
  103.6 23.2 %scatter_custom_fusion = f32[31,4096]{0,1:T(8,128)S(1)} fusion(s32[4096]{0:T(1024)S(1)} %get-tuple-element.21, f32[4096,31]{1,0:T(8,128)} %copy.142, f32[]{:T(128)} %constant.25.clone.1), kind=kCustom, calls=%fused_computation.10 | custom fusion | flops 126976 | bytes 508416 | tf_op jit(solution)/shard_map/scatter-add | solution.py:55
  126.8 1.4 copy.143
  128.2 21.3 %all_to_all.17 = f32[31,32,128]{2,0,1:T(8,128)S(1)} all-to-all(f32[31,32,128]{2,0,1:T(8,128)} %copy.143), channel_id=1, replica_groups=mesh['gx'=8,'gy'=4] {'gx','gy'}, dimensions={1} | all-to-all | bytes 1015808 | tf_op jit(solution)/shard_map/all_to_all | solution.py:56
  150.2 2.0 %copy.145 = f32[4096,31]{1,0:T(8,128)} copy(f32[4096,31]{0,1:T(8,128)S(1)} %bitcast.165) | data formatting | bytes 1015808 | tf_op jit(solution)/shard_map/all_to_all | solution.py:56
  152.2 22.9 %scatter_custom_fusion.1 = f32[31,2048]{0,1:T(8,128)S(1)} fusion(s32[4096]{0:T(1024)S(1)} %bitcast.169, f32[4096,31]{1,0:T(8,128)} %copy.145, f32[]{:T(128)} %constant.25.clone.1), kind=kCustom, calls=%fused_computation.23 | custom fusion | flops 126976 | bytes 254464 | tf_op jit(solution)/shard_map/scatter-add | solution.py:57
  175.1 0.6 fusion
  176.1 1.0 copy.146
  (64 shorter events, 20.6 us)
Async XLA Ops:
  0.6 18.3 %copy-start.2 = (f32[30,4,4,128]{3,2,1,0:T(4,128)S(1)}, f32[30,4,4,128]{3,2,1,0:T(4,128)}, u32[]{:S(2)}) copy-start(f32[30,4,4,128]{3,2,1,0:T(4,128)} %param.8) | copy-start | bytes 737284
  0.6 18.3 %copy-start.6 = (f32[4,4,128]{2,1,0:T(4,128)S(1)}, f32[4,4,128]{2,1,0:T(4,128)}, u32[]{:S(2)}) copy-start(f32[4,4,128]{2,1,0:T(4,128)} %param.9) | copy-start | bytes 24580
  1.6 7.7 %collective-permute-start.1 = (f32[30,1,4,128]{3,2,1,0:T(4,128)S(1)}, f32[30,1,4,128]{3,2,1,0:T(4,128)S(1)}, u32[]{:S(2)}, u32[]{:S(2)}) collective-permute-start(f32[30,1,4,128]{3,2,1,0:T(4,128)S(1)} %get-tuple-element.19), channel_id=1, source_target_pairs={{0,4},{4,8},{8,12},{12,16},{16,20},{20,24},{24,28},{1,5},{5,9},{9,... | collective-permute-start | bytes 184328 | tf_op jit(solution)/shard_map/ppermute | solution.py:16
  6.4 6.1 %collective-permute-start = (f32[30,1,4,128]{3,2,1,0:T(4,128)S(1)}, f32[30,1,4,128]{3,2,1,0:T(4,128)S(1)}, u32[]{:S(2)}, u32[]{:S(2)}) collective-permute-start(f32[30,1,4,128]{3,2,1,0:T(4,128)S(1)} %get-tuple-element.18), channel_id=1, source_target_pairs={{4,0},{8,4},{12,8},{16,12},{20,16},{24,20},{28,24},{5,1},{9,5},{13... | collective-permute-start | bytes 184328 | tf_op jit(solution)/shard_map/ppermute | solution.py:17
  12.7 4.4 %collective-permute-start.3 = (f32[30,6,1,128]{3,2,1,0:T(1,128)S(1)}, f32[30,6,1,128]{3,2,1,0:T(1,128)S(1)}, u32[]{:S(2)}, u32[]{:S(2)}) collective-permute-start(f32[30,6,1,128]{3,2,1,0:T(1,128)S(1)} %get-tuple-element.17), channel_id=1, source_target_pairs={{0,1},{1,2},{2,3},{4,5},{5,6},{6,7},{8,9},{9,10},{10,11},{12,13},{... | collective-permute-start | bytes 276488 | tf_op jit(solution)/shard_map/ppermute | solution.py:16
  14.0 4.9 %collective-permute-start.2 = (f32[30,6,1,128]{3,2,1,0:T(1,128)S(1)}, f32[30,6,1,128]{3,2,1,0:T(1,128)S(1)}, u32[]{:S(2)}, u32[]{:S(2)}) collective-permute-start(f32[30,6,1,128]{3,2,1,0:T(1,128)S(1)} %get-tuple-element.16), channel_id=1, source_target_pairs={{1,0},{2,1},{3,2},{5,4},{6,5},{7,6},{9,8},{10,9},{11,10},{13,12},{... | collective-permute-start | bytes 276488 | tf_op jit(solution)/shard_map/ppermute | solution.py:17
  55.8 26.6 %all-to-all-start = ((f32[32,31,128]{2,1,0:T(8,128)}), f32[32,31,128]{2,1,0:T(8,128)}, u32[]{:S(2)}, u32[]{:S(2)}) async-start(f32[32,31,128]{2,1,0:T(8,128)} %constant_dynamic-update-slice_fusion.3), calls=%async_computation | async-start | bytes 1048576 | tf_op jit(solution)/shard_map/all_to_all | solution.py:44
  79.3 3.0 %copy-start.4 = (s32[4096]{0:T(1024)S(1)}, s32[4096]{0:T(1024)}, u32[]{:S(2)}) copy-start(s32[4096]{0:T(1024)} %param.15) | copy-start | bytes 49156
  79.3 3.0 %copy-start.3 = (s32[4096]{0:T(1024)S(1)}, s32[4096]{0:T(1024)}, u32[]{:S(2)}) copy-start(s32[4096]{0:T(1024)} %param.14) | copy-start | bytes 49156
  98.2 2.4 %copy-start = (f32[30,4096]{1,0:T(8,128)S(1)}, f32[30,4096]{1,0:T(8,128)}, u32[]{:S(2)}) copy-start(f32[30,4096]{1,0:T(8,128)} %param.12) | copy-start | bytes 1474564
  98.2 2.4 %copy-start.1 = (f32[4096,30]{0,1:T(8,128)S(1)}, f32[4096,30]{0,1:T(8,128)}, u32[]{:S(2)}) copy-start(f32[4096,30]{0,1:T(8,128)} %copy.141) | copy-start | bytes 1474564
  98.2 2.4 %copy-start.5 = (f32[4096]{0:T(1024)S(1)}, f32[4096]{0:T(1024)}, u32[]{:S(2)}) copy-start(f32[4096]{0:T(1024)} %param.13) | copy-start | bytes 49156
